TPU v7x, 32 devices: a whole 2x2x4 slice. The times are simulated.
32 devices in a mesh: stack: 2 (over y), acq: 4 (over x, core), rng: 4 (over z).
Axes of the slice: x: 2, y: 2, z: 4, core: 2. Of those that a mesh axis runs over, the one named last changes fastest.
Arguments:
- images: bfloat16 [2, 16, 128, 1024], P(None, ('stack', 'acq'), None, 'rng'), parts along dimension 1, may hold values from -16 to 16
- pairing: int32 [3, 8], replicated, may hold values from 0 to 7, as said below
- tile_offsets: int32 [3, 2], replicated, may hold values from 0 to 31, as said below
Outputs:
- coherence: float32 [3, 16, 64, 1024], P(None, ('stack', 'acq'), None, 'rng'), parts along dimension 1
- filtered: bfloat16 [2, 3, 16, 64, 1024], P(None, None, ('stack', 'acq'), None, 'rng'), parts along dimension 2
There are 2 independent parts, one for each index of `stack`. A program takes and returns all parts, laid end to end along the dimension named above; an argument that names none is the same for every part. Nothing has to cross between parts.
Inputs may be any that keep to these rules, and one draw needn't show every extreme that they name: In matching m, the partner of acquisition a lies in group (a // 2) XOR (m + 1), and the pairing is an involution. `tile_offsets`: both ends occur in every draw.
All inputs are finite; a program needn't handle non-finite values.
Results may differ from a plain program's by a relative error of at most 0.001.
Values may be sent and summed in bfloat16 or wider, within the bound.
A program may use at most 64 MiB of HBM per device.

v0:
```python
import functools

import jax
import jax.numpy as jnp
import ml_dtypes
import numpy as np
from jax import lax
from jax.experimental import pallas as pl
from jax.experimental.pallas import tpu as pltpu
from jax.sharding import PartitionSpec as P

MATCH = 3
REACH = 32
PATCH = 32
EPSILON = 1e-06
LANES = 128
MESH = pl.DeviceIdType.MESH
BF16 = jnp.bfloat16
F32 = jnp.float32


def halves(table):
    high = table.astype(ml_dtypes.bfloat16)
    low = (table - high.astype(np.float64)).astype(ml_dtypes.bfloat16)
    return high, low


def gauss(distance):
    weights = np.exp(-(distance.astype(np.float64) ** 2) / (2.0 * (REACH / 8.0) ** 2))
    return np.where(np.abs(distance) <= REACH, weights, 0.0)


def range_table(breadth):
    lane = np.arange(breadth + LANES)
    cell = np.where(lane >= breadth + LANES - REACH, lane - breadth - LANES, lane)
    used = cell < breadth + REACH
    weights = gauss(cell[:, None] - np.arange(breadth)[None, :])
    return np.stack(halves(weights * used[:, None]))


def azimuth_table(height):
    line = np.arange(height)
    return np.stack(halves(gauss(line[:, None] - line[None, :])))


def column_tables():
    counter = np.arange(PATCH)
    angles = 2.0 * np.pi / PATCH * (counter[:, None] * counter[None, :] % PATCH)
    eye = np.eye(LANES // PATCH)
    cosine, sine = np.kron(eye, np.cos(angles)), np.kron(eye, np.sin(angles))
    there = np.block([[cosine, -sine], [sine, cosine]])
    back = np.block([[cosine, sine], [-sine, cosine]])
    return np.stack(halves(there) + halves(back))


def row_tables(height):
    line = np.arange(height)[None, :]
    frequency = np.arange(PATCH)[:, None]
    angles = 2.0 * np.pi / PATCH * (frequency * line % PATCH)
    cosine, sine = np.cos(angles), np.sin(angles)
    first = np.concatenate([cosine, sine], 1)
    second = np.concatenate([-sine, cosine], 1)
    there = np.stack([first, second]).astype(np.float32)
    count = height // PATCH + 1
    tiled = np.concatenate([np.tile(first, (count, 1)), np.tile(second, (count, 1))], 0)
    turned = np.concatenate([np.tile(second, (count, 1)), np.tile(-first, (count, 1))], 0)
    back = np.stack([tiled.T, turned.T]).astype(np.float32) / (PATCH * PATCH)
    offset = np.arange(PATCH)[None, :]
    angles = 2.0 * np.pi / PATCH * (frequency * offset % PATCH)
    turn = np.stack([np.cos(angles), np.sin(angles)]).astype(np.float32)
    turn_lanes = np.tile(turn.transpose(0, 2, 1), (1, 1, 2 * count))
    return there, back, turn, turn_lanes


def split(value):
    high = value.astype(BF16)
    return high, (value - high.astype(F32)).astype(BF16)


def times_table(value, high, low):
    value_high, value_low = split(value)
    return jnp.dot(
        jnp.concatenate([value_high, value_low, value_high], 1),
        jnp.concatenate([high, high, low], 0),
        preferred_element_type=F32,
    )


def table_times(high, low, value):
    value_high, value_low = split(value)
    return jnp.dot(
        jnp.concatenate([high, high, low], 1),
        jnp.concatenate([value_high, value_low, value_high], 0),
        preferred_element_type=F32,
    )


def chosen(index, table, axis):
    place = lax.broadcasted_iota(jnp.int32, table.shape, axis)
    return jnp.sum(jnp.where(place == index, table, 0.0), axis=axis, keepdims=True)


def pair_kernel(
    pairing,
    offsets,
    images_far,
    range_band_far,
    columns_far,
    azimuth_band,
    rows_there,
    rows_back,
    turn,
    turn_lanes,
    coherence,
    filtered,
    images,
    range_band,
    columns,
    mains,
    lefts,
    rights,
    own_left,
    own_right,
    heads,
    tails,
    send_sem,
    recv_sem,
    load_sem,
):
    stack, group, strip = lax.axis_index("stack"), lax.axis_index("acq"), lax.axis_index("rng")
    strips = lax.axis_size("rng")
    height = images.shape[2] // 2
    breadth = images.shape[3]
    wide = breadth + LANES
    near, far = jnp.bitwise_xor(group, 1), jnp.bitwise_xor(group, 2)
    has_left, has_right = strip > 0, strip < strips - 1

    loads = [
        pltpu.make_async_copy(source, target, load_sem.at[index])
        for index, (source, target) in enumerate(
            ((images_far, images), (range_band_far, range_band), (columns_far, columns))
        )
    ]
    loads[0].start()
    barrier = pltpu.get_barrier_semaphore()

    def greet(g, r):
        pl.semaphore_signal(barrier, inc=1, device_id=(stack, g, r), device_id_type=MESH)

    greet(near, strip)
    greet(far, strip)

    @pl.when(has_left)
    def _():
        for g in (group, near, far):
            greet(g, strip - 1)

    @pl.when(has_right)
    def _():
        for g in (group, near, far):
            greet(g, strip + 1)

    loads[1].start()
    loads[2].start()
    loads[0].wait()
    lane = lax.broadcasted_iota(jnp.int32, (2 * height, LANES), 1) // REACH
    head = jnp.zeros((2 * height, LANES), F32)
    tail = jnp.zeros((2 * height, LANES), F32)
    for part in range(2):
        for member in range(2):
            place = 2 * part + member
            first = images[part, member, :, :LANES].astype(F32)
            last = images[part, member, :, breadth - LANES :].astype(F32)
            if place:
                first = pltpu.roll(first, REACH * place, 1)
            if place != 3:
                last = pltpu.roll(last, REACH * (place + 1), 1)
            head = jnp.where(lane == place, first, head)
            tail = jnp.where(lane == place, last, tail)
    heads[...] = head.astype(BF16)
    tails[...] = tail.astype(BF16)

    pl.semaphore_wait(
        barrier, 2 + 3 * has_left.astype(jnp.int32) + 3 * has_right.astype(jnp.int32)
    )

    def copy(source, target, index, g, r):
        return pltpu.make_async_remote_copy(
            src_ref=source,
            dst_ref=target,
            send_sem=send_sem.at[index],
            recv_sem=recv_sem.at[index],
            device_id=(stack, g, r),
            device_id_type=MESH,
        )

    def rows(g):
        return pl.ds(pl.multiple_of((g > group).astype(jnp.int32) * height, height), height)

    main_far = copy(images.at[:, :, rows(far), :], mains.at[1], 0, far, strip)
    main_near = copy(images.at[:, :, rows(near), :], mains.at[0], 1, near, strip)
    right_far = copy(heads.at[rows(far), :], rights.at[1], 2, far, strip - 1)
    right_near = copy(heads.at[rows(near), :], rights.at[0], 3, near, strip - 1)
    right_own = copy(heads, own_right, 4, group, strip - 1)
    left_far = copy(tails.at[rows(far), :], lefts.at[1], 5, far, strip + 1)
    left_near = copy(tails.at[rows(near), :], lefts.at[0], 6, near, strip + 1)
    left_own = copy(tails, own_left, 7, group, strip + 1)
    main_on = copy(mains.at[1], mains.at[2], 8, near, strip)
    right_on = copy(rights.at[1], rights.at[2], 9, near, strip)
    left_on = copy(lefts.at[1], lefts.at[2], 10, near, strip)

    main_near.start()
    main_far.start()

    @pl.when(has_left)
    def _():
        right_near.start()
        right_own.start()
        right_far.start()

    @pl.when(has_right)
    def _():
        left_near.start()
        left_own.start()
        left_far.start()

    def arrive(main, left, right):
        @pl.when(has_left)
        def _():
            left.wait_recv()

        @pl.when(has_right)
        def _():
            right.wait_recv()

        main.wait_recv()

    work = functools.partial(
        pair_work,
        pairing,
        offsets,
        images,
        own_left,
        own_right,
        mains,
        lefts,
        rights,
        range_band,
        azimuth_band,
        columns,
        rows_there,
        rows_back,
        turn,
        turn_lanes,
        coherence,
        filtered,
    )

    def step(matching, carry):
        @pl.when(matching == 0)
        def _():
            @pl.when(has_left)
            def _():
                left_own.wait_recv()

            @pl.when(has_right)
            def _():
                right_own.wait_recv()

            arrive(main_near, left_near, right_near)
            loads[1].wait()
            loads[2].wait()

        @pl.when(matching == 1)
        def _():
            arrive(main_far, left_far, right_far)
            main_on.start()

            @pl.when(has_left)
            def _():
                left_on.start()

            @pl.when(has_right)
            def _():
                right_on.start()

        @pl.when(matching == 2)
        def _():
            arrive(main_on, left_on, right_on)

        work(matching)
        return carry

    lax.fori_loop(0, MATCH, step, 0)

    main_near.wait_send()
    main_far.wait_send()
    main_on.wait_send()

    @pl.when(has_left)
    def _():
        right_near.wait_send()
        right_own.wait_send()
        right_far.wait_send()
        left_on.wait_send()

    @pl.when(has_right)
    def _():
        left_near.wait_send()
        left_own.wait_send()
        left_far.wait_send()
        right_on.wait_send()


def pair_work(
    pairing,
    offsets,
    images,
    own_left,
    own_right,
    mains,
    lefts,
    rights,
    range_band,
    azimuth_band,
    columns,
    rows_there,
    rows_back,
    turn,
    turn_lanes,
    coherence,
    filtered,
    matching,
):
    group, strip = lax.axis_index("acq"), lax.axis_index("rng")
    has_left, has_right = strip > 0, strip < lax.axis_size("rng") - 1
    height, breadth = mains.shape[3], mains.shape[4]
    wide = breadth + LANES
    upper = (group > jnp.bitwise_xor(group, matching + 1)).astype(jnp.int32)
    lines = pl.ds(pl.multiple_of(upper * height, height), height)
    lane = lax.broadcasted_iota(jnp.int32, (height, LANES), 1)
    at_right = jnp.logical_and(lane < REACH, has_right)
    at_left = jnp.logical_and(lane >= LANES - REACH, has_left)

    def widened(main, left, right, place):
        if place:
            right = pltpu.roll(right, LANES - REACH * place, 1)
        if place != 3:
            left = pltpu.roll(left, LANES - REACH - REACH * place, 1)
        rim = jnp.where(at_right, right, jnp.where(at_left, left, 0.0))
        return jnp.concatenate([main.astype(F32), rim], 1)

    my_left, my_right = own_left[lines, :].astype(F32), own_right[lines, :].astype(F32)
    their_left, their_right = lefts[matching].astype(F32), rights[matching].astype(F32)
    crossed = lax.rem(pairing[matching, 2 * group], 2)
    crossed = jnp.broadcast_to(crossed, (height, wide)) == 1
    ours, others = [
        [
            [widened(main(part, member), left, right, 2 * part + member) for part in range(2)]
            for member in range(2)
        ]
        for main, left, right in (
            (lambda part, member: images[part, member, lines, :], my_left, my_right),
            (lambda part, member: mains[matching, part, member], their_left, their_right),
        )
    ]
    fields = []
    for member in range(2):
        mine = ours[member]
        theirs = [
            jnp.where(crossed, others[1 - member][part], others[member][part])
            for part in range(2)
        ]
        fields.append(
            [
                mine[0] * theirs[0] + mine[1] * theirs[1],
                mine[1] * theirs[0] - mine[0] * theirs[1],
                mine[0] * mine[0] + mine[1] * mine[1],
                theirs[0] * theirs[0] + theirs[1] * theirs[1],
            ]
        )

    smoothed = times_table(
        jnp.concatenate(fields[0] + fields[1], 0), range_band[0], range_band[1]
    )
    for member in range(2):
        real, imag, mine, theirs = [
            table_times(
                azimuth_band[0],
                azimuth_band[1],
                smoothed[(4 * member + f) * height : (4 * member + f + 1) * height],
            )
            for f in range(4)
        ]
        coherence[matching, member] = (real * real + imag * imag) / (mine * theirs + EPSILON)

    groups = breadth // LANES
    blocks = 2 * groups + 1
    count = height // PATCH + 1
    shift = REACH - offsets[1, matching]
    windows = [
        [pltpu.roll(fields[member][part], shift, 1) for part in range(2)] for member in range(2)
    ]
    cells = []
    for member in range(2):
        for block in range(groups):
            cells.append(
                jnp.concatenate(
                    [w[:, block * LANES : (block + 1) * LANES] for w in windows[member]], 1
                )
            )
    cells.append(
        jnp.concatenate(
            [
                jnp.where(
                    lane < PATCH,
                    windows[0][part][:, breadth:],
                    pltpu.roll(windows[1][part][:, breadth:], PATCH, 1),
                )
                for part in range(2)
            ],
            1,
        )
    )
    rowwise = times_table(jnp.concatenate(cells, 0), columns[0], columns[1])

    def upright(value):
        return jnp.concatenate(
            [
                jnp.concatenate(
                    [
                        value[b * height : (b + 1) * height, :LANES],
                        value[b * height : (b + 1) * height, LANES:],
                    ],
                    0,
                )
                for b in range(blocks)
            ],
            1,
        )

    def flat(value):
        return jnp.concatenate(
            [
                jnp.concatenate(
                    [
                        value[:height, b * LANES : (b + 1) * LANES],
                        value[height:, b * LANES : (b + 1) * LANES],
                    ],
                    1,
                )
                for b in range(blocks)
            ],
            0,
        )

    high = count * PATCH
    line_offset = offsets[0, matching]
    cosine, sine = [chosen(line_offset, turn[k], 1) for k in range(2)]
    upper_rows = rows_there[0] * cosine - rows_there[1] * sine
    lower_rows = rows_there[1] * cosine + rows_there[0] * sine
    line = lax.rem(lax.broadcasted_iota(jnp.int32, upper_rows.shape, 1), height)
    patch = (line - line_offset + PATCH) // PATCH
    there = jnp.concatenate(
        [
            jnp.where(patch == j, table, 0.0)
            for table in (upper_rows, lower_rows)
            for j in range(count)
        ],
        0,
    )
    frequency = table_times(*split(there), upright(rowwise))
    real, imag = frequency[:high], frequency[high:]
    magnitude = lax.rsqrt(lax.rsqrt(real * real + imag * imag + EPSILON))
    sums = [
        jnp.sum(magnitude[j * PATCH : (j + 1) * PATCH], axis=0, keepdims=True)
        for j in range(count)
    ]
    sums = jnp.concatenate(
        [s[:, b * LANES : (b + 1) * LANES] for b in range(blocks) for s in sums]
        + [jnp.zeros((-blocks * count % 8, LANES), F32)] * (blocks * count % 8 != 0),
        0,
    )
    first = lax.broadcasted_iota(jnp.int32, (LANES, LANES), 0) // PATCH
    second = lax.broadcasted_iota(jnp.int32, (LANES, LANES), 1) // PATCH
    ones = (first == second).astype(F32).astype(BF16)
    sums_high, sums_low = split(sums)
    total = jnp.dot(
        jnp.concatenate([sums_high, sums_low], 1),
        jnp.concatenate([ones, ones], 0),
        preferred_element_type=F32,
    )
    inverse = 1.0 / (total * (1.0 / (PATCH * PATCH)) + EPSILON)
    scaling = jnp.concatenate(
        [
            jnp.concatenate(
                [
                    magnitude[j * PATCH : (j + 1) * PATCH, b * LANES : (b + 1) * LANES]
                    * inverse[b * count + j : b * count + j + 1]
                    for j in range(count)
                ],
                0,
            )
            for b in range(blocks)
        ],
        1,
    )
    weighted = jnp.concatenate([real * scaling, imag * scaling], 0)
    cosine, sine = [chosen(line_offset, turn_lanes[k], 0) for k in range(2)]
    back_rows = rows_back[0] * cosine - rows_back[1] * sine
    line = lax.rem(lax.broadcasted_iota(jnp.int32, back_rows.shape, 0), height)
    patch = (line - line_offset + PATCH) // PATCH
    place = lax.rem(lax.broadcasted_iota(jnp.int32, back_rows.shape, 1), high) // PATCH
    back_rows = jnp.where(patch == place, back_rows, 0.0)
    back = table_times(*split(back_rows), weighted)
    final = times_table(flat(back), columns[2], columns[3])
    rim = final[2 * groups * height :]
    for member in range(2):
        for part in range(2):
            pieces = [
                final[b * height : (b + 1) * height, part * LANES : (part + 1) * LANES]
                for b in range(member * groups, (member + 1) * groups)
            ]
            last = rim[:, part * LANES : (part + 1) * LANES]
            if member:
                last = pltpu.roll(last, LANES - PATCH, 1)
            whole = pltpu.roll(jnp.concatenate(pieces + [last], 1), wide - shift, 1)
            filtered[part, matching, member] = whole[:, :breadth].astype(BF16)


def per_device(images, pairing, tile_offsets):
    height, breadth = images.shape[2] // 2, images.shape[3]
    tables = [range_table(breadth), column_tables(), azimuth_table(height)]
    tables += row_tables(height)
    vmem, smem = pl.BlockSpec(memory_space=pltpu.VMEM), pl.BlockSpec(memory_space=pltpu.SMEM)
    anywhere = pl.BlockSpec(memory_space=pl.ANY)
    results = [
        pltpu.VMEM((MATCH, 2, height, breadth), F32),
        pltpu.VMEM((2, MATCH, 2, height, breadth), BF16),
    ]
    operands = [pairing, tile_offsets.T, images] + [jnp.asarray(table) for table in tables]
    operands = [pltpu.with_memory_space_constraint(array, pltpu.HBM) for array in operands]
    return pl.pallas_call(
        pair_kernel,
        in_specs=[smem] * 2 + [anywhere] * 3 + [vmem] * 5,
        out_specs=[vmem] * 2,
        out_shape=results,
        scratch_shapes=[
            pltpu.VMEM(images.shape, BF16),
            pltpu.VMEM(tables[0].shape, BF16),
            pltpu.VMEM(tables[1].shape, BF16),
            pltpu.VMEM((MATCH, 2, 2, height, breadth), BF16),
            pltpu.VMEM((MATCH, height, LANES), BF16),
            pltpu.VMEM((MATCH, height, LANES), BF16),
            pltpu.VMEM((2 * height, LANES), BF16),
            pltpu.VMEM((2 * height, LANES), BF16),
            pltpu.VMEM((2 * height, LANES), BF16),
            pltpu.VMEM((2 * height, LANES), BF16),
            pltpu.SemaphoreType.DMA((11,)),
            pltpu.SemaphoreType.DMA((11,)),
            pltpu.SemaphoreType.DMA((3,)),
        ],
        compiler_params=pltpu.CompilerParams(
            collective_id=0, has_side_effects=True, vmem_limit_bytes=40 * 2**20
        ),
        name="pairs",
    )(*operands)


def solution(mesh):
    in_specs = (P(None, ("stack", "acq"), None, "rng"), P(), P())
    out_specs = (
        P(None, ("stack", "acq"), None, "rng"),
        P(None, None, ("stack", "acq"), None, "rng"),
    )
    return jax.shard_map(
        per_device, mesh=mesh, in_specs=in_specs, out_specs=out_specs, check_vma=False
    )
```

profile of v0, /device:TPU:0, one launch (start us, length us, event | category | flops | bytes accessed | tf_op | source)
XLA Modules:
  0.0 18.6 jit_solution(6698316957455614442)
XLA Ops:
  0.6 16.5 %pairs.1 = (f32[3,2,64,256]{3,2,1,0:T(8,128)S(1)}, bf16[2,3,2,64,256]{4,3,2,1,0:T(8,128)(2,1)S(1)}) custom-call(s32[3,8]{1,0:T(4,128)} %pairing.1, s32[2,3]{1,0:T(2,128)} %bitcast.1, bf16[2,2,128,256]{3,2,1,0:T(8,128)(2,1)} %images_far.1, bf16[2,384,256]{2,1,0:T(8,128)(2,1)} %constant.14.clone.range_band_far, ...), custom_call_target="tpu_custom_call" | custom-call | tf_op jit(solution)/shard_map/pairs/pallas_call | solution.py:543
  17.1 0.7 %copy.14 = f32[3,2,64,256]{3,2,1,0:T(8,128)} copy(f32[3,2,64,256]{3,2,1,0:T(8,128)S(1)} %get-tuple-element.2) | data formatting | bytes 786432
  17.9 0.7 %copy.15 = bf16[2,3,2,64,256]{4,3,2,1,0:T(8,128)(2,1)} copy(bf16[2,3,2,64,256]{4,3,2,1,0:T(8,128)(2,1)S(1)} %get-tuple-element.3) | data formatting | bytes 786432
where the time goes:
time: 18.8 us; the launch traced here: 18.6 us
  Pallas kernels  16.5 us (88%)
  local copies, waits for them, and re-layouts  1.49 us (8%)
  between operations  0.64 us (3%)
    pallas_call x1, Pallas kernels, per_device(): pl.pallas_call(pair_kernel, in_specs=[smem] * 2 + [anywhere] * 3 + [vmem]...  16.5 us
    unnamed x2, local copies, waits for them, and re-layouts  1.49 us

commit v1 on v0

--- a/solution.py
+++ b/solution.py
@@ -87,12 +87,21 @@
 
 
 def table_times(high, low, value):
+    count, depth = high.shape
     value_high, value_low = split(value)
-    return jnp.dot(
-        jnp.concatenate([high, high, low], 1),
-        jnp.concatenate([value_high, value_low, value_high], 0),
-        preferred_element_type=F32,
-    )
+    if depth <= LANES:
+        lower = jnp.concatenate([low, jnp.zeros_like(low)], 1)
+        both = jnp.dot(
+            jnp.concatenate([jnp.concatenate([high, high], 1), lower], 0),
+            jnp.concatenate([value_high, value_low], 0),
+            preferred_element_type=F32,
+        )
+        return both[:count] + both[count:]
+    both = jnp.dot(
+        jnp.concatenate([high, low], 0), value_high, preferred_element_type=F32
+    )
+    rest = jnp.dot(high, value_low, preferred_element_type=F32)
+    return both[:count] + both[count:] + rest
 
 
 def chosen(index, table, axis):
@@ -383,17 +392,6 @@
     smoothed = times_table(
         jnp.concatenate(fields[0] + fields[1], 0), range_band[0], range_band[1]
     )
-    for member in range(2):
-        real, imag, mine, theirs = [
-            table_times(
-                azimuth_band[0],
-                azimuth_band[1],
-                smoothed[(4 * member + f) * height : (4 * member + f + 1) * height],
-            )
-            for f in range(4)
-        ]
-        coherence[matching, member] = (real * real + imag * imag) / (mine * theirs + EPSILON)
-
     groups = breadth // LANES
     blocks = 2 * groups + 1
     count = height // PATCH + 1
@@ -423,6 +421,12 @@
         )
     )
     rowwise = times_table(jnp.concatenate(cells, 0), columns[0], columns[1])
+    spread = [
+        table_times(
+            azimuth_band[0], azimuth_band[1], smoothed[f * height : (f + 1) * height]
+        )
+        for f in range(8)
+    ]
 
     def upright(value):
         return jnp.concatenate(
@@ -470,6 +474,10 @@
         0,
     )
     frequency = table_times(*split(there), upright(rowwise))
+    for member in range(2):
+        real, imag, mine, theirs = spread[4 * member : 4 * member + 4]
+        coherence[matching, member] = (real * real + imag * imag) / (mine * theirs + EPSILON)
+
     real, imag = frequency[:high], frequency[high:]
     magnitude = lax.rsqrt(lax.rsqrt(real * real + imag * imag + EPSILON))
     sums = [

time: 18.8 us -> 18.3 us (0.973)
  Pallas kernels: 16.5 us -> 16 us
    pallas_call x1, Pallas kernels: 16.5 us -> 16 us  [per_device(): pl.pallas_call(pair_kernel, in_specs=[smem] * 2 + [anywhere] * 3 + [vmem]...]
where the time goes in v1:
time: 18.3 us; the launch traced here: 18.2 us
  Pallas kernels  16 us (87%)
  local copies, waits for them, and re-layouts  1.49 us (8%)
  between operations  0.64 us (3%)
    pallas_call x1, Pallas kernels, per_device(): pl.pallas_call(pair_kernel, in_specs=[smem] * 2 + [anywhere] * 3 + [vmem]...  16 us
    unnamed x2, local copies, waits for them, and re-layouts  1.49 us

profile of v1, /device:TPU:0, one launch (start us, length us, event | category | flops | bytes accessed | tf_op | source)
XLA Modules:
  0.0 18.2 jit_solution(146497440195658756)
XLA Ops:
  0.6 16.0 %pairs.1 = (f32[3,2,64,256]{3,2,1,0:T(8,128)S(1)}, bf16[2,3,2,64,256]{4,3,2,1,0:T(8,128)(2,1)S(1)}) custom-call(s32[3,8]{1,0:T(4,128)} %pairing.1, s32[2,3]{1,0:T(2,128)} %bitcast.1, bf16[2,2,128,256]{3,2,1,0:T(8,128)(2,1)} %images_far.1, bf16[2,384,256]{2,1,0:T(8,128)(2,1)} %constant.14.clone.range_band_far, ...), custom_call_target="tpu_custom_call" | custom-call | tf_op jit(solution)/shard_map/pairs/pallas_call | solution.py:551
  16.7 0.7 %copy.14 = f32[3,2,64,256]{3,2,1,0:T(8,128)} copy(f32[3,2,64,256]{3,2,1,0:T(8,128)S(1)} %get-tuple-element.2) | data formatting | bytes 786432
  17.4 0.7 %copy.15 = bf16[2,3,2,64,256]{4,3,2,1,0:T(8,128)(2,1)} copy(bf16[2,3,2,64,256]{4,3,2,1,0:T(8,128)(2,1)S(1)} %get-tuple-element.3) | data formatting | bytes 786432

commit v2 on v1

--- a/solution.py
+++ b/solution.py
@@ -1,5 +1,3 @@
-import functools
-
 import jax
 import jax.numpy as jnp
 import ml_dtypes
@@ -109,46 +107,34 @@
     return jnp.sum(jnp.where(place == index, table, 0.0), axis=axis, keepdims=True)
 
 
-def pair_kernel(
-    pairing,
-    offsets,
+TABLES = ("range_band", "columns", "azimuth_band", "rows_there", "rows_back", "turn", "turn_lanes")
+
+
+def first_kernel(
+    pairing_far,
+    offsets_far,
     images_far,
-    range_band_far,
-    columns_far,
-    azimuth_band,
-    rows_there,
-    rows_back,
-    turn,
-    turn_lanes,
-    coherence,
-    filtered,
-    images,
-    range_band,
-    columns,
-    mains,
-    lefts,
-    rights,
-    own_left,
-    own_right,
-    heads,
-    tails,
-    send_sem,
-    recv_sem,
-    load_sem,
+    *refs,
 ):
+    tables_far, refs = refs[: len(TABLES)], refs[len(TABLES) :]
+    (coherence, filtered, power, images, own_left, own_right, main_last, left_last, right_last), refs = (
+        refs[:9],
+        refs[9:],
+    )
+    tables, refs = refs[: len(TABLES)], refs[len(TABLES) :]
+    pairing, offsets, mains, lefts, rights, heads, tails, send_sem, recv_sem, load_sem = refs
     stack, group, strip = lax.axis_index("stack"), lax.axis_index("acq"), lax.axis_index("rng")
     strips = lax.axis_size("rng")
     height = images.shape[2] // 2
     breadth = images.shape[3]
-    wide = breadth + LANES
     near, far = jnp.bitwise_xor(group, 1), jnp.bitwise_xor(group, 2)
     has_left, has_right = strip > 0, strip < strips - 1
 
+    pairs = [(images_far, images), (pairing_far, pairing), (offsets_far, offsets)]
+    pairs += list(zip(tables_far, tables))
     loads = [
         pltpu.make_async_copy(source, target, load_sem.at[index])
-        for index, (source, target) in enumerate(
-            ((images_far, images), (range_band_far, range_band), (columns_far, columns))
-        )
+        for index, (source, target) in enumerate(pairs)
     ]
     loads[0].start()
     barrier = pltpu.get_barrier_semaphore()
@@ -169,8 +155,8 @@
         for g in (group, near, far):
             greet(g, strip + 1)
 
-    loads[1].start()
-    loads[2].start()
+    for load in loads[1:]:
+        load.start()
     loads[0].wait()
     lane = lax.broadcasted_iota(jnp.int32, (2 * height, LANES), 1) // REACH
     head = jnp.zeros((2 * height, LANES), F32)
@@ -214,9 +200,9 @@
     left_far = copy(tails.at[rows(far), :], lefts.at[1], 5, far, strip + 1)
     left_near = copy(tails.at[rows(near), :], lefts.at[0], 6, near, strip + 1)
     left_own = copy(tails, own_left, 7, group, strip + 1)
-    main_on = copy(mains.at[1], mains.at[2], 8, near, strip)
-    right_on = copy(rights.at[1], rights.at[2], 9, near, strip)
-    left_on = copy(lefts.at[1], lefts.at[2], 10, near, strip)
+    main_on = copy(mains.at[1], main_last, 8, near, strip)
+    right_on = copy(rights.at[1], right_last, 9, near, strip)
+    left_on = copy(lefts.at[1], left_last, 10, near, strip)
 
     main_near.start()
     main_far.start()
@@ -243,27 +229,6 @@
             right.wait_recv()
 
         main.wait_recv()
-
-    work = functools.partial(
-        pair_work,
-        pairing,
-        offsets,
-        images,
-        own_left,
-        own_right,
-        mains,
-        lefts,
-        rights,
-        range_band,
-        azimuth_band,
-        columns,
-        rows_there,
-        rows_back,
-        turn,
-        turn_lanes,
-        coherence,
-        filtered,
-    )
 
     def step(matching, carry):
         @pl.when(matching == 0)
@@ -277,8 +242,8 @@
                 right_own.wait_recv()
 
             arrive(main_near, left_near, right_near)
-            loads[1].wait()
-            loads[2].wait()
+            for load in loads[1:]:
+                load.wait()
 
         @pl.when(matching == 1)
         def _():
@@ -293,15 +258,27 @@
             def _():
                 right_on.start()
 
-        @pl.when(matching == 2)
-        def _():
-            arrive(main_on, left_on, right_on)
-
-        work(matching)
+        pair_work(
+            pairing,
+            offsets,
+            images,
+            own_left,
+            own_right,
+            mains.at[matching],
+            lefts.at[matching],
+            rights.at[matching],
+            tables,
+            coherence.at[matching],
+            filtered.at[:, matching],
+            power,
+            matching,
+            False,
+        )
         return carry
 
-    lax.fori_loop(0, MATCH, step, 0)
-
+    lax.fori_loop(0, MATCH - 1, step, 0)
+
+    arrive(main_on, left_on, right_on)
     main_near.wait_send()
     main_far.wait_send()
     main_on.wait_send()
@@ -321,29 +298,83 @@
         right_on.wait_send()
 
 
+def last_kernel(
+    pairing,
+    offsets,
+    coherence_first,
+    filtered_first,
+    power,
+    images,
+    own_left,
+    own_right,
+    main_last,
+    left_last,
+    right_last,
+    *refs,
+):
+    tables, refs = refs[: len(TABLES)], refs[len(TABLES) :]
+    coherence_far, filtered_far, coherence, filtered, early_sem, late_sem = refs
+    last = MATCH - 1
+    early = [
+        pltpu.make_async_copy(
+            coherence_first.at[m], coherence_far.at[m], early_sem.at[0, m]
+        )
+        for m in range(last)
+    ] + [
+        pltpu.make_async_copy(
+            filtered_first.at[:, m], filtered_far.at[:, m], early_sem.at[1, m]
+        )
+        for m in range(last)
+    ]
+    late = [
+        pltpu.make_async_copy(coherence, coherence_far.at[last], late_sem.at[0]),
+        pltpu.make_async_copy(filtered, filtered_far.at[:, last], late_sem.at[1]),
+    ]
+    for store in early:
+        store.start()
+    pair_work(
+        pairing,
+        offsets,
+        images,
+        own_left,
+        own_right,
+        main_last,
+        left_last,
+        right_last,
+        tables,
+        coherence,
+        filtered,
+        power,
+        last,
+        True,
+        late[0].start,
+    )
+    late[1].start()
+    for store in early + late:
+        store.wait()
+
+
 def pair_work(
     pairing,
     offsets,
     images,
     own_left,
     own_right,
-    mains,
-    lefts,
-    rights,
-    range_band,
-    azimuth_band,
-    columns,
-    rows_there,
-    rows_back,
-    turn,
-    turn_lanes,
+    main,
+    left,
+    right,
+    tables,
     coherence,
     filtered,
+    power,
     matching,
+    known,
+    stored=lambda: None,
 ):
+    range_band, columns, azimuth_band, rows_there, rows_back, turn, turn_lanes = tables
     group, strip = lax.axis_index("acq"), lax.axis_index("rng")
     has_left, has_right = strip > 0, strip < lax.axis_size("rng") - 1
-    height, breadth = mains.shape[3], mains.shape[4]
+    height, breadth = main.shape[2], main.shape[3]
     wide = breadth + LANES
     upper = (group > jnp.bitwise_xor(group, matching + 1)).astype(jnp.int32)
     lines = pl.ds(pl.multiple_of(upper * height, height), height)
@@ -360,17 +391,17 @@
         return jnp.concatenate([main.astype(F32), rim], 1)
 
     my_left, my_right = own_left[lines, :].astype(F32), own_right[lines, :].astype(F32)
-    their_left, their_right = lefts[matching].astype(F32), rights[matching].astype(F32)
+    their_left, their_right = left[...].astype(F32), right[...].astype(F32)
     crossed = lax.rem(pairing[matching, 2 * group], 2)
     crossed = jnp.broadcast_to(crossed, (height, wide)) == 1
     ours, others = [
         [
-            [widened(main(part, member), left, right, 2 * part + member) for part in range(2)]
+            [widened(source(part, member), left, right, 2 * part + member) for part in range(2)]
             for member in range(2)
         ]
-        for main, left, right in (
+        for source, left, right in (
             (lambda part, member: images[part, member, lines, :], my_left, my_right),
-            (lambda part, member: mains[matching, part, member], their_left, their_right),
+            (lambda part, member: main[part, member], their_left, their_right),
         )
     ]
     fields = []
@@ -384,9 +415,9 @@
             [
                 mine[0] * theirs[0] + mine[1] * theirs[1],
                 mine[1] * theirs[0] - mine[0] * theirs[1],
-                mine[0] * mine[0] + mine[1] * mine[1],
                 theirs[0] * theirs[0] + theirs[1] * theirs[1],
             ]
+            + ([] if known else [mine[0] * mine[0] + mine[1] * mine[1]])
         )
 
     smoothed = times_table(
@@ -425,7 +456,7 @@
         table_times(
             azimuth_band[0], azimuth_band[1], smoothed[f * height : (f + 1) * height]
         )
-        for f in range(8)
+        for f in range(2 * len(fields[0]))
     ]
 
     def upright(value):
@@ -475,8 +506,13 @@
     )
     frequency = table_times(*split(there), upright(rowwise))
     for member in range(2):
-        real, imag, mine, theirs = spread[4 * member : 4 * member + 4]
-        coherence[matching, member] = (real * real + imag * imag) / (mine * theirs + EPSILON)
+        count_fields = len(fields[0])
+        real, imag, theirs = spread[count_fields * member : count_fields * member + 3]
+        mine = power[member] if known else spread[count_fields * member + 3]
+        if not known:
+            power[member] = mine
+        coherence[member] = (real * real + imag * imag) / (mine * theirs + EPSILON)
+    stored()
 
     real, imag = frequency[:high], frequency[high:]
     magnitude = lax.rsqrt(lax.rsqrt(real * real + imag * imag + EPSILON))
@@ -533,46 +569,70 @@
             if member:
                 last = pltpu.roll(last, LANES - PATCH, 1)
             whole = pltpu.roll(jnp.concatenate(pieces + [last], 1), wide - shift, 1)
-            filtered[part, matching, member] = whole[:, :breadth].astype(BF16)
+            filtered[part, member] = whole[:, :breadth].astype(BF16)
 
 
 def per_device(images, pairing, tile_offsets):
     height, breadth = images.shape[2] // 2, images.shape[3]
     tables = [range_table(breadth), column_tables(), azimuth_table(height)]
     tables += row_tables(height)
+    offsets = tile_offsets.T
     vmem, smem = pl.BlockSpec(memory_space=pltpu.VMEM), pl.BlockSpec(memory_space=pltpu.SMEM)
     anywhere = pl.BlockSpec(memory_space=pl.ANY)
-    results = [
-        pltpu.VMEM((MATCH, 2, height, breadth), F32),
-        pltpu.VMEM((2, MATCH, 2, height, breadth), BF16),
-    ]
-    operands = [pairing, tile_offsets.T, images] + [jnp.asarray(table) for table in tables]
+    operands = [pairing, offsets, images] + [jnp.asarray(table) for table in tables]
     operands = [pltpu.with_memory_space_constraint(array, pltpu.HBM) for array in operands]
-    return pl.pallas_call(
-        pair_kernel,
-        in_specs=[smem] * 2 + [anywhere] * 3 + [vmem] * 5,
-        out_specs=[vmem] * 2,
-        out_shape=results,
+    slab, halo = (2, 2, height, breadth), (height, LANES)
+    between = [
+        pltpu.VMEM((MATCH - 1, 2, height, breadth), F32),
+        pltpu.VMEM((2, MATCH - 1, 2, height, breadth), BF16),
+        pltpu.VMEM((2, height, breadth), F32),
+        pltpu.VMEM(images.shape, BF16),
+        pltpu.VMEM((2 * height, LANES), BF16),
+        pltpu.VMEM((2 * height, LANES), BF16),
+        pltpu.VMEM(slab, BF16),
+        pltpu.VMEM(halo, BF16),
+        pltpu.VMEM(halo, BF16),
+    ] + [pltpu.VMEM(table.shape, jnp.dtype(table.dtype)) for table in tables]
+    held = pl.pallas_call(
+        first_kernel,
+        in_specs=[anywhere] * len(operands),
+        out_specs=[vmem] * len(between),
+        out_shape=between,
         scratch_shapes=[
-            pltpu.VMEM(images.shape, BF16),
-            pltpu.VMEM(tables[0].shape, BF16),
-            pltpu.VMEM(tables[1].shape, BF16),
-            pltpu.VMEM((MATCH, 2, 2, height, breadth), BF16),
-            pltpu.VMEM((MATCH, height, LANES), BF16),
-            pltpu.VMEM((MATCH, height, LANES), BF16),
-            pltpu.VMEM((2 * height, LANES), BF16),
-            pltpu.VMEM((2 * height, LANES), BF16),
+            pltpu.SMEM(pairing.shape, jnp.int32),
+            pltpu.SMEM(offsets.shape, jnp.int32),
+            pltpu.VMEM((MATCH - 1,) + slab, BF16),
+            pltpu.VMEM((MATCH - 1,) + halo, BF16),
+            pltpu.VMEM((MATCH - 1,) + halo, BF16),
             pltpu.VMEM((2 * height, LANES), BF16),
             pltpu.VMEM((2 * height, LANES), BF16),
             pltpu.SemaphoreType.DMA((11,)),
             pltpu.SemaphoreType.DMA((11,)),
-            pltpu.SemaphoreType.DMA((3,)),
+            pltpu.SemaphoreType.DMA((len(operands),)),
         ],
         compiler_params=pltpu.CompilerParams(
             collective_id=0, has_side_effects=True, vmem_limit_bytes=40 * 2**20
         ),
-        name="pairs",
+        name="first",
     )(*operands)
+    held = [pltpu.with_memory_space_constraint(array, pltpu.VMEM) for array in held]
+    return pl.pallas_call(
+        last_kernel,
+        in_specs=[smem] * 2 + [vmem] * len(held),
+        out_specs=[anywhere] * 2,
+        out_shape=[
+            jax.ShapeDtypeStruct((MATCH, 2, height, breadth), F32),
+            jax.ShapeDtypeStruct((2, MATCH, 2, height, breadth), BF16),
+        ],
+        scratch_shapes=[
+            pltpu.VMEM((2, height, breadth), F32),
+            pltpu.VMEM(slab, BF16),
+            pltpu.SemaphoreType.DMA((2, MATCH - 1)),
+            pltpu.SemaphoreType.DMA((2,)),
+        ],
+        compiler_params=pltpu.CompilerParams(vmem_limit_bytes=40 * 2**20),
+        name="last",
+    )(*operands[:2], *held)
 
 
 def solution(mesh):

time: 18.3 us -> 17.2 us (0.940)
  local copies, waits for them, and re-layouts: 1.49 us -> 0 us
  Pallas kernels: 16 us -> 16.4 us
    unnamed x2 -> x0, local copies, waits for them, and re-layouts: 1.49 us -> none
    pallas_call x1 -> x2, Pallas kernels: 16 us -> 16.4 us  [the longest x1 12.8 us: per_device(): pl.pallas_call(first_kernel, in_specs=[anywhere] * len(operands), out_spe...]
where the time goes in v2:
time: 17.2 us; the launch traced here: 17 us
  Pallas kernels  16.4 us (95%)
  between operations  0.64 us (4%)
    pallas_call x1, Pallas kernels, per_device(): pl.pallas_call(first_kernel, in_specs=[anywhere] * len(operands), out_spe...  12.8 us
    pallas_call x1, Pallas kernels, per_device(): pl.pallas_call(last_kernel, in_specs=[smem] * 2 + [vmem] * len(held), out...  3.58 us

profile of v2, /device:TPU:0, one launch (start us, length us, event | category | flops | bytes accessed | tf_op | source)
XLA Modules:
  0.0 17.0 jit_solution(10208804926920049561)
XLA Ops:
  0.6 12.8 %first.1 = (f32[2,2,64,256]{3,2,1,0:T(8,128)S(1)}, bf16[2,2,2,64,256]{4,3,2,1,0:T(8,128)(2,1)S(1)}, f32[2,64,256]{2,1,0:T(8,128)S(1)}, bf16[2,2,128,256]{3,2,1,0...) custom-call(s32[3,8]{1,0:T(4,128)} %pairing.1, ...), custom_call_target="tpu_custom_call" | custom-call | tf_op jit(solution)/shard_map/first/pallas_call | solution.py:596
  13.4 3.6 %last.1 = (f32[3,2,64,256]{3,2,1,0:T(8,128)}, bf16[2,3,2,64,256]{4,3,2,1,0:T(8,128)(2,1)}) custom-call(s32[3,8]{1,0:T(4,128)} %pairing.1, s32[2,3]{1,0:T(2,128)} %bitcast.2, f32[2,2,64,256]{3,2,1,0:T(8,128)S(1)} %get-tuple-element.18.coherence_first, bf16[2,2,2,64,256]{4,3,2,1,0:T(8,128)(2,1)S(1)} %get-tuple-element.19.filtered_first, ...), custom_call_target="tpu_custom_call" | custom-call | tf_op jit(solution)/shard_map/last/pallas_call | solution.py:619

commit v3 on v2

--- a/solution.py
+++ b/solution.py
@@ -168,10 +168,9 @@
             last = images[part, member, :, breadth - LANES :].astype(F32)
             if place:
                 first = pltpu.roll(first, REACH * place, 1)
-            if place != 3:
-                last = pltpu.roll(last, REACH * (place + 1), 1)
+                last = pltpu.roll(last, REACH * place, 1)
             head = jnp.where(lane == place, first, head)
-            tail = jnp.where(lane == place, last, tail)
+            tail = jnp.where(lane == (place + 3) % 4, last, tail)
     heads[...] = head.astype(BF16)
     tails[...] = tail.astype(BF16)
 
@@ -379,15 +378,14 @@
     upper = (group > jnp.bitwise_xor(group, matching + 1)).astype(jnp.int32)
     lines = pl.ds(pl.multiple_of(upper * height, height), height)
     lane = lax.broadcasted_iota(jnp.int32, (height, LANES), 1)
-    at_right = jnp.logical_and(lane < REACH, has_right)
-    at_left = jnp.logical_and(lane >= LANES - REACH, has_left)
+    slot = lane // REACH
 
     def widened(main, left, right, place):
+        at_right = jnp.logical_and(slot == place, has_right)
+        at_left = jnp.logical_and(slot == (place + 3) % 4, has_left)
+        rim = jnp.where(at_right, right, jnp.where(at_left, left, 0.0))
         if place:
-            right = pltpu.roll(right, LANES - REACH * place, 1)
-        if place != 3:
-            left = pltpu.roll(left, LANES - REACH - REACH * place, 1)
-        rim = jnp.where(at_right, right, jnp.where(at_left, left, 0.0))
+            rim = pltpu.roll(rim, LANES - REACH * place, 1)
         return jnp.concatenate([main.astype(F32), rim], 1)
 
     my_left, my_right = own_left[lines, :].astype(F32), own_right[lines, :].astype(F32)
@@ -423,28 +421,59 @@
     smoothed = times_table(
         jnp.concatenate(fields[0] + fields[1], 0), range_band[0], range_band[1]
     )
+
+    def spread(member):
+        count_fields = len(fields[0])
+        results = [
+            table_times(
+                azimuth_band[0],
+                azimuth_band[1],
+                smoothed[(count_fields * member + f) * height :][:height],
+            )
+            for f in range(count_fields)
+        ]
+        if known:
+            results.append(power[member])
+        else:
+            power[member] = results[3]
+        return results
+
+    def finish(member, results):
+        real, imag, theirs, mine = results
+        coherence[member] = (real * real + imag * imag) / (mine * theirs + EPSILON)
+
     groups = breadth // LANES
-    blocks = 2 * groups + 1
     count = height // PATCH + 1
+    high = count * PATCH
+    line_offset = offsets[0, matching]
     shift = REACH - offsets[1, matching]
-    windows = [
-        [pltpu.roll(fields[member][part], shift, 1) for part in range(2)] for member in range(2)
+
+    def window(field):
+        turned = [
+            pltpu.roll(field[:, g * LANES : (g + 1) * LANES], shift, 1)
+            for g in range(groups + 1)
+        ]
+        return [jnp.where(lane < shift, turned[g - 1], turned[g]) for g in range(groups + 1)]
+
+    def unwindow(pieces):
+        turned = [pltpu.roll(piece, LANES - shift, 1) for piece in pieces]
+        return jnp.concatenate(
+            [jnp.where(lane < LANES - shift, turned[g], turned[g + 1]) for g in range(groups)], 1
+        )
+
+    windows = [[window(fields[member][part]) for part in range(2)] for member in range(2)]
+    cells = [
+        jnp.concatenate([windows[member][part][block] for part in range(2)], 1)
+        for member in range(2)
+        for block in range(groups)
     ]
-    cells = []
-    for member in range(2):
-        for block in range(groups):
-            cells.append(
-                jnp.concatenate(
-                    [w[:, block * LANES : (block + 1) * LANES] for w in windows[member]], 1
-                )
-            )
     cells.append(
         jnp.concatenate(
             [
                 jnp.where(
                     lane < PATCH,
-                    windows[0][part][:, breadth:],
-                    pltpu.roll(windows[1][part][:, breadth:], PATCH, 1),
+                    windows[0][part][groups],
+                    pltpu.roll(windows[1][part][groups], PATCH, 1),
                 )
                 for part in range(2)
             ],
@@ -452,20 +481,73 @@
         )
     )
     rowwise = times_table(jnp.concatenate(cells, 0), columns[0], columns[1])
-    spread = [
-        table_times(
-            azimuth_band[0], azimuth_band[1], smoothed[f * height : (f + 1) * height]
-        )
-        for f in range(2 * len(fields[0]))
-    ]
-
-    def upright(value):
-        return jnp.concatenate(
+
+    cosine, sine = [chosen(line_offset, turn[k], 1) for k in range(2)]
+    upper_rows = rows_there[0] * cosine - rows_there[1] * sine
+    lower_rows = rows_there[1] * cosine + rows_there[0] * sine
+    line = lax.rem(lax.broadcasted_iota(jnp.int32, upper_rows.shape, 1), height)
+    patch = (line - line_offset + PATCH) // PATCH
+    there = split(
+        jnp.concatenate(
+            [
+                jnp.where(patch == j, table, 0.0)
+                for table in (upper_rows, lower_rows)
+                for j in range(count)
+            ],
+            0,
+        )
+    )
+    cosine, sine = [chosen(line_offset, turn_lanes[k], 0) for k in range(2)]
+    back_rows = rows_back[0] * cosine - rows_back[1] * sine
+    line = lax.rem(lax.broadcasted_iota(jnp.int32, back_rows.shape, 0), height)
+    patch = (line - line_offset + PATCH) // PATCH
+    place = lax.rem(lax.broadcasted_iota(jnp.int32, back_rows.shape, 1), high) // PATCH
+    back_again = split(jnp.where(patch == place, back_rows, 0.0))
+
+    first = lax.broadcasted_iota(jnp.int32, (2 * LANES, LANES), 0) % LANES // PATCH
+    second = lax.broadcasted_iota(jnp.int32, (2 * LANES, LANES), 1) // PATCH
+    ones = (first == second).astype(F32).astype(BF16)
+
+    def transformed(blocks):
+        upright = jnp.concatenate(
             [
                 jnp.concatenate(
                     [
-                        value[b * height : (b + 1) * height, :LANES],
-                        value[b * height : (b + 1) * height, LANES:],
+                        rowwise[b * height : (b + 1) * height, :LANES],
+                        rowwise[b * height : (b + 1) * height, LANES:],
+                    ],
+                    0,
+                )
+                for b in blocks
+            ],
+            1,
+        )
+        return table_times(*there, upright)
+
+    def reweighted(frequency):
+        blocks = frequency.shape[1] // LANES
+        real, imag = frequency[:high], frequency[high:]
+        magnitude = lax.rsqrt(lax.rsqrt(real * real + imag * imag + EPSILON))
+        sums = [
+            jnp.sum(magnitude[j * PATCH : (j + 1) * PATCH], axis=0, keepdims=True)
+            for j in range(count)
+        ]
+        sums = [s[:, b * LANES : (b + 1) * LANES] for b in range(blocks) for s in sums]
+        if len(sums) % 8:
+            sums.append(jnp.zeros((-len(sums) % 8, LANES), F32))
+        total = jnp.dot(
+            jnp.concatenate(split(jnp.concatenate(sums, 0)), 1),
+            ones,
+            preferred_element_type=F32,
+        )
+        inverse = 1.0 / (total * (1.0 / (PATCH * PATCH)) + EPSILON)
+        scaling = jnp.concatenate(
+            [
+                jnp.concatenate(
+                    [
+                        magnitude[j * PATCH : (j + 1) * PATCH, b * LANES : (b + 1) * LANES]
+                        * inverse[b * count + j : b * count + j + 1]
+                        for j in range(count)
                     ],
                     0,
                 )
@@ -473,103 +555,42 @@
             ],
             1,
         )
-
-    def flat(value):
-        return jnp.concatenate(
-            [
-                jnp.concatenate(
-                    [
-                        value[:height, b * LANES : (b + 1) * LANES],
-                        value[height:, b * LANES : (b + 1) * LANES],
-                    ],
-                    1,
-                )
-                for b in range(blocks)
-            ],
-            0,
-        )
-
-    high = count * PATCH
-    line_offset = offsets[0, matching]
-    cosine, sine = [chosen(line_offset, turn[k], 1) for k in range(2)]
-    upper_rows = rows_there[0] * cosine - rows_there[1] * sine
-    lower_rows = rows_there[1] * cosine + rows_there[0] * sine
-    line = lax.rem(lax.broadcasted_iota(jnp.int32, upper_rows.shape, 1), height)
-    patch = (line - line_offset + PATCH) // PATCH
-    there = jnp.concatenate(
-        [
-            jnp.where(patch == j, table, 0.0)
-            for table in (upper_rows, lower_rows)
-            for j in range(count)
-        ],
-        0,
-    )
-    frequency = table_times(*split(there), upright(rowwise))
-    for member in range(2):
-        count_fields = len(fields[0])
-        real, imag, theirs = spread[count_fields * member : count_fields * member + 3]
-        mine = power[member] if known else spread[count_fields * member + 3]
-        if not known:
-            power[member] = mine
-        coherence[member] = (real * real + imag * imag) / (mine * theirs + EPSILON)
-    stored()
-
-    real, imag = frequency[:high], frequency[high:]
-    magnitude = lax.rsqrt(lax.rsqrt(real * real + imag * imag + EPSILON))
-    sums = [
-        jnp.sum(magnitude[j * PATCH : (j + 1) * PATCH], axis=0, keepdims=True)
-        for j in range(count)
-    ]
-    sums = jnp.concatenate(
-        [s[:, b * LANES : (b + 1) * LANES] for b in range(blocks) for s in sums]
-        + [jnp.zeros((-blocks * count % 8, LANES), F32)] * (blocks * count % 8 != 0),
-        0,
-    )
-    first = lax.broadcasted_iota(jnp.int32, (LANES, LANES), 0) // PATCH
-    second = lax.broadcasted_iota(jnp.int32, (LANES, LANES), 1) // PATCH
-    ones = (first == second).astype(F32).astype(BF16)
-    sums_high, sums_low = split(sums)
-    total = jnp.dot(
-        jnp.concatenate([sums_high, sums_low], 1),
-        jnp.concatenate([ones, ones], 0),
-        preferred_element_type=F32,
-    )
-    inverse = 1.0 / (total * (1.0 / (PATCH * PATCH)) + EPSILON)
-    scaling = jnp.concatenate(
-        [
+        return jnp.concatenate([real * scaling, imag * scaling], 0)
+
+    def returned(weighted):
+        back = table_times(*back_again, weighted)
+        return [
             jnp.concatenate(
                 [
-                    magnitude[j * PATCH : (j + 1) * PATCH, b * LANES : (b + 1) * LANES]
-                    * inverse[b * count + j : b * count + j + 1]
-                    for j in range(count)
+                    back[:height, b * LANES : (b + 1) * LANES],
+                    back[height:, b * LANES : (b + 1) * LANES],
                 ],
-                0,
+                1,
             )
-            for b in range(blocks)
-        ],
-        1,
-    )
-    weighted = jnp.concatenate([real * scaling, imag * scaling], 0)
-    cosine, sine = [chosen(line_offset, turn_lanes[k], 0) for k in range(2)]
-    back_rows = rows_back[0] * cosine - rows_back[1] * sine
-    line = lax.rem(lax.broadcasted_iota(jnp.int32, back_rows.shape, 0), height)
-    patch = (line - line_offset + PATCH) // PATCH
-    place = lax.rem(lax.broadcasted_iota(jnp.int32, back_rows.shape, 1), high) // PATCH
-    back_rows = jnp.where(patch == place, back_rows, 0.0)
-    back = table_times(*split(back_rows), weighted)
-    final = times_table(flat(back), columns[2], columns[3])
-    rim = final[2 * groups * height :]
+            for b in range(weighted.shape[1] // LANES)
+        ]
+
+    chains = [range(groups), range(groups, 2 * groups), range(2 * groups, 2 * groups + 1)]
+    frequency = [transformed(chains[0]), transformed(chains[1])]
+    results = spread(0)
+    flat = returned(reweighted(frequency[0]))
+    frequency.append(transformed(chains[2]))
+    finish(0, results)
+    flat += returned(reweighted(frequency[1]))
+    results = spread(1)
+    flat += returned(reweighted(frequency[2]))
+    finish(1, results)
+    stored()
+    final = times_table(jnp.concatenate(flat, 0), columns[2], columns[3])
     for member in range(2):
         for part in range(2):
             pieces = [
                 final[b * height : (b + 1) * height, part * LANES : (part + 1) * LANES]
-                for b in range(member * groups, (member + 1) * groups)
+                for b in [*chains[member], 2 * groups]
             ]
-            last = rim[:, part * LANES : (part + 1) * LANES]
             if member:
-                last = pltpu.roll(last, LANES - PATCH, 1)
-            whole = pltpu.roll(jnp.concatenate(pieces + [last], 1), wide - shift, 1)
-            filtered[part, member] = whole[:, :breadth].astype(BF16)
+                pieces[-1] = pltpu.roll(pieces[-1], LANES - PATCH, 1)
+            filtered[part, member] = unwindow(pieces).astype(BF16)
 
 
 def per_device(images, pairing, tile_offsets):

time: 17.2 us -> 16.7 us (0.971)
  Pallas kernels: 16.4 us -> 15.9 us
    pallas_call x1, Pallas kernels: 12.8 us -> 12.4 us  [per_device(): pl.pallas_call(first_kernel, in_specs=[anywhere] * len(operands), out_spe...]
where the time goes in v3:
time: 16.7 us; the launch traced here: 16.5 us
  Pallas kernels  15.9 us (95%)
  between operations  0.64 us (4%)
    pallas_call x1, Pallas kernels, per_device(): pl.pallas_call(first_kernel, in_specs=[anywhere] * len(operands), out_spe...  12.4 us
    pallas_call x1, Pallas kernels, per_device(): pl.pallas_call(last_kernel, in_specs=[smem] * 2 + [vmem] * len(held), out...  3.51 us

profile of v3, /device:TPU:0, one launch (start us, length us, event | category | flops | bytes accessed | tf_op | source)
XLA Modules:
  0.0 16.5 jit_solution(10936865017971097375)
XLA Ops:
  0.6 12.4 %first.1 = (f32[2,2,64,256]{3,2,1,0:T(8,128)S(1)}, bf16[2,2,2,64,256]{4,3,2,1,0:T(8,128)(2,1)S(1)}, f32[2,64,256]{2,1,0:T(8,128)S(1)}, bf16[2,2,128,256]{3,2,1,0...) custom-call(s32[3,8]{1,0:T(4,128)} %pairing.1, ...), custom_call_target="tpu_custom_call" | custom-call | tf_op jit(solution)/shard_map/first/pallas_call | solution.py:617
  13.0 3.5 %last.1 = (f32[3,2,64,256]{3,2,1,0:T(8,128)}, bf16[2,3,2,64,256]{4,3,2,1,0:T(8,128)(2,1)}) custom-call(s32[3,8]{1,0:T(4,128)} %pairing.1, s32[2,3]{1,0:T(2,128)} %bitcast.2, f32[2,2,64,256]{3,2,1,0:T(8,128)S(1)} %get-tuple-element.18.coherence_first, bf16[2,2,2,64,256]{4,3,2,1,0:T(8,128)(2,1)S(1)} %get-tuple-element.19.filtered_first, ...), custom_call_target="tpu_custom_call" | custom-call | tf_op jit(solution)/shard_map/last/pallas_call | solution.py:640

commit v4 on v3

--- a/solution.py
+++ b/solution.py
@@ -67,7 +67,16 @@
     angles = 2.0 * np.pi / PATCH * (frequency * offset % PATCH)
     turn = np.stack([np.cos(angles), np.sin(angles)]).astype(np.float32)
     turn_lanes = np.tile(turn.transpose(0, 2, 1), (1, 1, 2 * count))
-    return there, back, turn, turn_lanes
+    patch = np.arange(2 * count * PATCH)[:, None] // PATCH % count
+    place = np.arange(2 * height)[None, :] % height + PATCH - PATCH * patch
+    place = place.astype(np.float32)
+    return there, back, turn, turn_lanes, place, np.ascontiguousarray(place.T)
+
+
+def sum_table():
+    first = np.arange(2 * LANES)[:, None] % LANES // PATCH
+    second = np.arange(LANES)[None, :] // PATCH
+    return (first == second).astype(ml_dtypes.bfloat16)
 
 
 def split(value):
@@ -107,7 +116,7 @@
     return jnp.sum(jnp.where(place == index, table, 0.0), axis=axis, keepdims=True)
 
 
-TABLES = ("range_band", "columns", "azimuth_band", "rows_there", "rows_back", "turn", "turn_lanes")
+TABLES = 10
 
 
 def first_kernel(
@@ -116,12 +125,12 @@
     images_far,
     *refs,
 ):
-    tables_far, refs = refs[: len(TABLES)], refs[len(TABLES) :]
+    tables_far, refs = refs[: TABLES], refs[TABLES :]
     (coherence, filtered, power, images, own_left, own_right, main_last, left_last, right_last), refs = (
         refs[:9],
         refs[9:],
     )
-    tables, refs = refs[: len(TABLES)], refs[len(TABLES) :]
+    tables, refs = refs[: TABLES], refs[TABLES :]
     pairing, offsets, mains, lefts, rights, heads, tails, send_sem, recv_sem, load_sem = refs
     stack, group, strip = lax.axis_index("stack"), lax.axis_index("acq"), lax.axis_index("rng")
     strips = lax.axis_size("rng")
@@ -158,7 +167,8 @@
     for load in loads[1:]:
         load.start()
     loads[0].wait()
-    lane = lax.broadcasted_iota(jnp.int32, (2 * height, LANES), 1) // REACH
+    lane = lax.broadcasted_iota(jnp.int32, (2 * height, LANES), 1)
+    lane = lax.shift_right_logical(lane, REACH.bit_length() - 1)
     head = jnp.zeros((2 * height, LANES), F32)
     tail = jnp.zeros((2 * height, LANES), F32)
     for part in range(2):
@@ -311,7 +321,7 @@
     right_last,
     *refs,
 ):
-    tables, refs = refs[: len(TABLES)], refs[len(TABLES) :]
+    tables, refs = refs[: TABLES], refs[TABLES :]
     coherence_far, filtered_far, coherence, filtered, early_sem, late_sem = refs
     last = MATCH - 1
     early = [
@@ -370,7 +380,8 @@
     known,
     stored=lambda: None,
 ):
-    range_band, columns, azimuth_band, rows_there, rows_back, turn, turn_lanes = tables
+    range_band, columns, azimuth_band, ones, rows_there, rows_back, turn, turn_lanes = tables[:8]
+    place_there, place_back = tables[8:]
     group, strip = lax.axis_index("acq"), lax.axis_index("rng")
     has_left, has_right = strip > 0, strip < lax.axis_size("rng") - 1
     height, breadth = main.shape[2], main.shape[3]
@@ -378,7 +389,7 @@
     upper = (group > jnp.bitwise_xor(group, matching + 1)).astype(jnp.int32)
     lines = pl.ds(pl.multiple_of(upper * height, height), height)
     lane = lax.broadcasted_iota(jnp.int32, (height, LANES), 1)
-    slot = lane // REACH
+    slot = lax.shift_right_logical(lane, REACH.bit_length() - 1)
 
     def widened(main, left, right, place):
         at_right = jnp.logical_and(slot == place, has_right)
@@ -485,28 +496,18 @@
     cosine, sine = [chosen(line_offset, turn[k], 1) for k in range(2)]
     upper_rows = rows_there[0] * cosine - rows_there[1] * sine
     lower_rows = rows_there[1] * cosine + rows_there[0] * sine
-    line = lax.rem(lax.broadcasted_iota(jnp.int32, upper_rows.shape, 1), height)
-    patch = (line - line_offset + PATCH) // PATCH
-    there = split(
-        jnp.concatenate(
-            [
-                jnp.where(patch == j, table, 0.0)
-                for table in (upper_rows, lower_rows)
-                for j in range(count)
-            ],
-            0,
-        )
-    )
+    line_start = line_offset.astype(F32)
+
+    def inside(place, table):
+        from_start = place[...] - line_start
+        return jnp.where(
+            jnp.logical_and(from_start >= 0.0, from_start < PATCH), table, 0.0
+        )
+
+    tall = jnp.concatenate([upper_rows] * count + [lower_rows] * count, 0)
+    there = split(inside(place_there, tall))
     cosine, sine = [chosen(line_offset, turn_lanes[k], 0) for k in range(2)]
-    back_rows = rows_back[0] * cosine - rows_back[1] * sine
-    line = lax.rem(lax.broadcasted_iota(jnp.int32, back_rows.shape, 0), height)
-    patch = (line - line_offset + PATCH) // PATCH
-    place = lax.rem(lax.broadcasted_iota(jnp.int32, back_rows.shape, 1), high) // PATCH
-    back_again = split(jnp.where(patch == place, back_rows, 0.0))
-
-    first = lax.broadcasted_iota(jnp.int32, (2 * LANES, LANES), 0) % LANES // PATCH
-    second = lax.broadcasted_iota(jnp.int32, (2 * LANES, LANES), 1) // PATCH
-    ones = (first == second).astype(F32).astype(BF16)
+    back_again = split(inside(place_back, rows_back[0] * cosine - rows_back[1] * sine))
 
     def transformed(blocks):
         upright = jnp.concatenate(
@@ -537,7 +538,7 @@
             sums.append(jnp.zeros((-len(sums) % 8, LANES), F32))
         total = jnp.dot(
             jnp.concatenate(split(jnp.concatenate(sums, 0)), 1),
-            ones,
+            ones[...],
             preferred_element_type=F32,
         )
         inverse = 1.0 / (total * (1.0 / (PATCH * PATCH)) + EPSILON)
@@ -595,7 +596,7 @@
 
 def per_device(images, pairing, tile_offsets):
     height, breadth = images.shape[2] // 2, images.shape[3]
-    tables = [range_table(breadth), column_tables(), azimuth_table(height)]
+    tables = [range_table(breadth), column_tables(), azimuth_table(height), sum_table()]
     tables += row_tables(height)
     offsets = tile_offsets.T
     vmem, smem = pl.BlockSpec(memory_space=pltpu.VMEM), pl.BlockSpec(memory_space=pltpu.SMEM)

time: 16.7 us -> 16.6 us (level)
  no operation moved by 1% of the time
where the time goes in v4:
time: 16.6 us; the launch traced here: 16.5 us
  Pallas kernels  15.8 us (95%)
  between operations  0.64 us (4%)
    pallas_call x1, Pallas kernels, per_device(): pl.pallas_call(first_kernel, in_specs=[anywhere] * len(operands), out_spe...  12.3 us
    pallas_call x1, Pallas kernels, per_device(): pl.pallas_call(last_kernel, in_specs=[smem] * 2 + [vmem] * len(held), out...  3.5 us

profile of v4, /device:TPU:0, one launch (start us, length us, event | category | flops | bytes accessed | tf_op | source)
XLA Modules:
  0.0 16.5 jit_solution(16657673572134786783)
XLA Ops:
  0.6 12.3 %first.1 = (f32[2,2,64,256]{3,2,1,0:T(8,128)S(1)}, bf16[2,2,2,64,256]{4,3,2,1,0:T(8,128)(2,1)S(1)}, f32[2,64,256]{2,1,0:T(8,128)S(1)}, bf16[2,2,128,256]{3,2,1,0...) custom-call(s32[3,8]{1,0:T(4,128)} %pairing.1, ...), custom_call_target="tpu_custom_call" | custom-call | tf_op jit(solution)/shard_map/first/pallas_call | solution.py:618
  13.0 3.5 %last.1 = (f32[3,2,64,256]{3,2,1,0:T(8,128)}, bf16[2,3,2,64,256]{4,3,2,1,0:T(8,128)(2,1)}) custom-call(s32[3,8]{1,0:T(4,128)} %pairing.1, s32[2,3]{1,0:T(2,128)} %bitcast.2, f32[2,2,64,256]{3,2,1,0:T(8,128)S(1)} %get-tuple-element.21.coherence_first, bf16[2,2,2,64,256]{4,3,2,1,0:T(8,128)(2,1)S(1)} %get-tuple-element.22.filtered_first, ...), custom_call_target="tpu_custom_call" | custom-call | tf_op jit(solution)/shard_map/last/pallas_call | solution.py:641

commit v5 on v4

--- a/solution.py
+++ b/solution.py
@@ -130,7 +130,8 @@
         refs[:9],
         refs[9:],
     )
-    tables, refs = refs[: TABLES], refs[TABLES :]
+    tables, refs = refs[:TABLES], refs[TABLES:]
+    there_rows, back_rows, *refs = refs
     pairing, offsets, mains, lefts, rights, heads, tails, send_sem, recv_sem, load_sem = refs
     stack, group, strip = lax.axis_index("stack"), lax.axis_index("acq"), lax.axis_index("rng")
     strips = lax.axis_size("rng")
@@ -228,6 +229,11 @@
         left_own.start()
         left_far.start()
 
+    for load in loads[1:]:
+        load.wait()
+    for matching in range(MATCH):
+        build_rows(offsets, tables, there_rows, back_rows, matching)
+
     def arrive(main, left, right):
         @pl.when(has_left)
         def _():
@@ -251,8 +257,6 @@
                 right_own.wait_recv()
 
             arrive(main_near, left_near, right_near)
-            for load in loads[1:]:
-                load.wait()
 
         @pl.when(matching == 1)
         def _():
@@ -277,6 +281,8 @@
             lefts.at[matching],
             rights.at[matching],
             tables,
+            there_rows,
+            back_rows,
             coherence.at[matching],
             filtered.at[:, matching],
             power,
@@ -322,6 +328,7 @@
     *refs,
 ):
     tables, refs = refs[: TABLES], refs[TABLES :]
+    there_rows, back_rows, *refs = refs
     coherence_far, filtered_far, coherence, filtered, early_sem, late_sem = refs
     last = MATCH - 1
     early = [
@@ -351,6 +358,8 @@
         left_last,
         right_last,
         tables,
+        there_rows,
+        back_rows,
         coherence,
         filtered,
         power,
@@ -361,6 +370,28 @@
     late[1].start()
     for store in early + late:
         store.wait()
+
+
+def build_rows(offsets, tables, there_rows, back_rows, matching):
+    rows_there, rows_back, turn, turn_lanes, place_there, place_back = tables[4:]
+    line_offset = offsets[0, matching]
+    cosine, sine = [chosen(line_offset, turn[k], 1) for k in range(2)]
+    upper_rows = rows_there[0] * cosine - rows_there[1] * sine
+    lower_rows = rows_there[1] * cosine + rows_there[0] * sine
+    line_start = line_offset.astype(F32)
+
+    def inside(place, table):
+        from_start = place[...] - line_start
+        return jnp.where(
+            jnp.logical_and(from_start >= 0.0, from_start < PATCH), table, 0.0
+        )
+
+    count = place_there.shape[0] // (2 * PATCH)
+    tall = jnp.concatenate([upper_rows] * count + [lower_rows] * count, 0)
+    there_rows[matching, 0], there_rows[matching, 1] = split(inside(place_there, tall))
+    cosine, sine = [chosen(line_offset, turn_lanes[k], 0) for k in range(2)]
+    turned = rows_back[0] * cosine - rows_back[1] * sine
+    back_rows[matching, 0], back_rows[matching, 1] = split(inside(place_back, turned))
 
 
 def pair_work(
@@ -373,6 +404,8 @@
     left,
     right,
     tables,
+    there_rows,
+    back_rows,
     coherence,
     filtered,
     power,
@@ -380,8 +413,7 @@
     known,
     stored=lambda: None,
 ):
-    range_band, columns, azimuth_band, ones, rows_there, rows_back, turn, turn_lanes = tables[:8]
-    place_there, place_back = tables[8:]
+    range_band, columns, azimuth_band, ones = tables[:4]
     group, strip = lax.axis_index("acq"), lax.axis_index("rng")
     has_left, has_right = strip > 0, strip < lax.axis_size("rng") - 1
     height, breadth = main.shape[2], main.shape[3]
@@ -456,7 +488,6 @@
     groups = breadth // LANES
     count = height // PATCH + 1
     high = count * PATCH
-    line_offset = offsets[0, matching]
     shift = REACH - offsets[1, matching]
 
     def window(field):
@@ -493,21 +524,8 @@
     )
     rowwise = times_table(jnp.concatenate(cells, 0), columns[0], columns[1])
 
-    cosine, sine = [chosen(line_offset, turn[k], 1) for k in range(2)]
-    upper_rows = rows_there[0] * cosine - rows_there[1] * sine
-    lower_rows = rows_there[1] * cosine + rows_there[0] * sine
-    line_start = line_offset.astype(F32)
-
-    def inside(place, table):
-        from_start = place[...] - line_start
-        return jnp.where(
-            jnp.logical_and(from_start >= 0.0, from_start < PATCH), table, 0.0
-        )
-
-    tall = jnp.concatenate([upper_rows] * count + [lower_rows] * count, 0)
-    there = split(inside(place_there, tall))
-    cosine, sine = [chosen(line_offset, turn_lanes[k], 0) for k in range(2)]
-    back_again = split(inside(place_back, rows_back[0] * cosine - rows_back[1] * sine))
+    there = (there_rows[matching, 0], there_rows[matching, 1])
+    back_again = (back_rows[matching, 0], back_rows[matching, 1])
 
     def transformed(blocks):
         upright = jnp.concatenate(
@@ -615,6 +633,8 @@
         pltpu.VMEM(halo, BF16),
         pltpu.VMEM(halo, BF16),
     ] + [pltpu.VMEM(table.shape, jnp.dtype(table.dtype)) for table in tables]
+    deep, high = 2 * height, 2 * (height + PATCH)
+    between += [pltpu.VMEM((MATCH, 2, high, deep), BF16), pltpu.VMEM((MATCH, 2, deep, high), BF16)]
     held = pl.pallas_call(
         first_kernel,
         in_specs=[anywhere] * len(operands),

time: 16.6 us -> 16.6 us (level)
  no operation moved by 1% of the time
where the time goes in v5:
time: 16.6 us; the launch traced here: 16.4 us
  Pallas kernels  15.8 us (95%)
  between operations  0.64 us (4%)
    pallas_call x1, Pallas kernels, per_device(): pl.pallas_call(first_kernel, in_specs=[anywhere] * len(operands), out_spe...  12.3 us
    pallas_call x1, Pallas kernels, per_device(): pl.pallas_call(last_kernel, in_specs=[smem] * 2 + [vmem] * len(held), out...  3.49 us

profile of v5, /device:TPU:0, one launch (start us, length us, event | category | flops | bytes accessed | tf_op | source)
XLA Modules:
  0.0 16.4 jit_solution(8042751116418083327)
XLA Ops:
  0.6 12.3 %first.1 = (f32[2,2,64,256]{3,2,1,0:T(8,128)S(1)}, bf16[2,2,2,64,256]{4,3,2,1,0:T(8,128)(2,1)S(1)}, f32[2,64,256]{2,1,0:T(8,128)S(1)}, bf16[2,2,128,256]{3,2,1,0...) custom-call(s32[3,8]{1,0:T(4,128)} %pairing.1, ...), custom_call_target="tpu_custom_call" | custom-call | tf_op jit(solution)/shard_map/first/pallas_call | solution.py:638
  12.9 3.5 %last.1 = (f32[3,2,64,256]{3,2,1,0:T(8,128)}, bf16[2,3,2,64,256]{4,3,2,1,0:T(8,128)(2,1)}) custom-call(s32[3,8]{1,0:T(4,128)} %pairing.1, s32[2,3]{1,0:T(2,128)} %bitcast.2, f32[2,2,64,256]{3,2,1,0:T(8,128)S(1)} %get-tuple-element.23.coherence_first, bf16[2,2,2,64,256]{4,3,2,1,0:T(8,128)(2,1)S(1)} %get-tuple-element.24.filtered_first, ...), custom_call_target="tpu_custom_call" | custom-call | tf_op jit(solution)/shard_map/last/pallas_call | solution.py:661

commit v6 on v5

--- a/solution.py
+++ b/solution.py
@@ -291,7 +291,8 @@
         )
         return carry
 
-    lax.fori_loop(0, MATCH - 1, step, 0)
+    for matching in range(MATCH - 1):
+        step(matching, 0)
 
     arrive(main_on, left_on, right_on)
     main_near.wait_send()

time: 16.6 us -> 16.5 us (level)
  no operation moved by 1% of the time
where the time goes in v6:
time: 16.5 us; the launch traced here: 16.3 us
  Pallas kernels  15.7 us (95%)
  between operations  0.64 us (4%)
    pallas_call x1, Pallas kernels, per_device(): pl.pallas_call(first_kernel, in_specs=[anywhere] * len(operands), out_spe...  12.2 us
    pallas_call x1, Pallas kernels, per_device(): pl.pallas_call(last_kernel, in_specs=[smem] * 2 + [vmem] * len(held), out...  3.49 us

profile of v6, /device:TPU:0, one launch (start us, length us, event | category | flops | bytes accessed | tf_op | source)
XLA Modules:
  0.0 16.3 jit_solution(9820692630872858802)
XLA Ops:
  0.6 12.2 %first.1 = (f32[2,2,64,256]{3,2,1,0:T(8,128)S(1)}, bf16[2,2,2,64,256]{4,3,2,1,0:T(8,128)(2,1)S(1)}, f32[2,64,256]{2,1,0:T(8,128)S(1)}, bf16[2,2,128,256]{3,2,1,0...) custom-call(s32[3,8]{1,0:T(4,128)} %pairing.1, ...), custom_call_target="tpu_custom_call" | custom-call | tf_op jit(solution)/shard_map/first/pallas_call | solution.py:639
  12.8 3.5 %last.1 = (f32[3,2,64,256]{3,2,1,0:T(8,128)}, bf16[2,3,2,64,256]{4,3,2,1,0:T(8,128)(2,1)}) custom-call(s32[3,8]{1,0:T(4,128)} %pairing.1, s32[2,3]{1,0:T(2,128)} %bitcast.2, f32[2,2,64,256]{3,2,1,0:T(8,128)S(1)} %get-tuple-element.23.coherence_first, bf16[2,2,2,64,256]{4,3,2,1,0:T(8,128)(2,1)S(1)} %get-tuple-element.24.filtered_first, ...), custom_call_target="tpu_custom_call" | custom-call | tf_op jit(solution)/shard_map/last/pallas_call | solution.py:662
